TPU v7x, 32 devices: a whole 2x2x4 slice. The times are simulated.
32 devices in a mesh: row: 4 (over y, core), col: 8 (over z, x).
Axes of the slice: x: 2, y: 2, z: 4, core: 2. Of those that a mesh axis runs over, the one named last changes fastest.
Arguments:
- kernel: float32 [4, 4, 256, 2, 8, 256], P(None, 'row', None, None, 'col'), as said below
- targets: float32 [4, 4, 256, 512], P(None, 'row', None, 'col'), may hold values from -6 to 6
Outputs:
- factored: float32 [4, 4, 256, 2, 8, 256], P(None, 'row', None, None, 'col')
- solved_targets: float32 [4, 4, 256, 512], P(None, 'row', None, 'col')
Inputs may be any that keep to these rules, and one draw needn't show every extreme that they name: kernel is symmetric positive definite with eigenvalues between about 0.5 and 38.
All inputs are finite; a program needn't handle non-finite values.
Results may differ from a plain program's by a relative error of at most 0.0001.
Values sent between devices are 32-bit elements; how exact they have to be, the bound alone decides.
A program may use at most 64 MiB of HBM per device.

v0:
```python
import functools

import jax
import jax.numpy as jnp
from jax import lax
from jax.experimental import pallas as pl
from jax.experimental.pallas import tpu as pltpu
from jax.sharding import PartitionSpec as P

STEP = 8
BASE = 128


def exact_dot(a, b, dims):
    return lax.dot_general(
        a, b, (dims, ((), ())), precision=lax.Precision.HIGHEST, preferred_element_type=jnp.float32
    )


def halves(a):
    high = a.astype(jnp.bfloat16)
    low = (a - high.astype(jnp.float32)).astype(jnp.bfloat16)
    return high, low


def split_dot(a, b, dims):
    def dot(x, y):
        return lax.dot_general(x, y, (dims, ((), ())), preferred_element_type=jnp.float32)

    a_high, a_low = a
    b_high, b_low = b
    return dot(a_high, b_high) + (dot(a_high, b_low) + dot(a_low, b_high))


def base_inverse(block):
    groups = BASE // STEP
    rows = lax.broadcasted_iota(jnp.int32, (STEP, BASE), 0)
    lanes = lax.broadcasted_iota(jnp.int32, (STEP, BASE), 1)
    full = (STEP, BASE)
    main = [block[STEP * p : STEP * (p + 1), :] for p in range(groups)]
    side = [(lanes == rows + STEP * p).astype(jnp.float32) for p in range(groups)]
    done = []
    for q in range(groups):
        here = main[q]
        first = STEP * q
        columns = [jnp.broadcast_to(here[:, first + j : first + j + 1], full) for j in range(STEP)]
        spot = [
            [jnp.broadcast_to(columns[j][i : i + 1, :], full) if i <= j else None for j in range(STEP)]
            for i in range(STEP)
        ]
        mains = [jnp.broadcast_to(here[i : i + 1, :], full) for i in range(STEP)]
        sides = [jnp.broadcast_to(side[q][i : i + 1, :], full) for i in range(STEP)]
        ratio = [[None] * STEP for _ in range(STEP)]
        recips = []
        for k in range(STEP):
            recip = 1.0 / spot[k][k]
            recips.append(recip)
            for i in range(k + 1, STEP):
                ratio[k][i] = spot[k][i] * recip
            for i in range(k + 1, STEP):
                for j in range(i, STEP):
                    spot[i][j] = spot[i][j] - ratio[k][i] * spot[k][j]
                mains[i] = mains[i] - ratio[k][i] * mains[k]
                sides[i] = sides[i] - ratio[k][i] * sides[k]
        scaled = jnp.zeros(full, jnp.float32)
        for k in range(STEP):
            scaled = jnp.where(rows == k, sides[k] * lax.rsqrt(spot[k][k]), scaled)
        done.append(scaled)
        if q == groups - 1:
            break
        mains = [mains[k] * recips[k] for k in range(STEP)]
        sides = [sides[k] * recips[k] for k in range(STEP)]
        for k in range(STEP - 1, 0, -1):
            for i in range(k):
                mains[i] = mains[i] - ratio[i][k] * mains[k]
                sides[i] = sides[i] - ratio[i][k] * sides[k]
        for p in range(q + 1, groups):
            factor = [
                jnp.broadcast_to(main[p][:, first + k : first + k + 1], full) for k in range(STEP)
            ]
            for target, source in ((main, mains), (side, sides)):
                terms = [factor[k] * source[k] for k in range(STEP)]
                while len(terms) > 1:
                    terms = [terms[t] + terms[t + 1] for t in range(0, len(terms), 2)]
                target[p] = target[p] - terms[0]
    return jnp.concatenate(done, axis=0)


MESH = pl.DeviceIdType.MESH
LANES = 128


def spread_kernel(
    nb, flat_ref, rhs_ref, rows_ref, corner_ref, head_ref,
    send_a, recv_a, send_b, recv_b, head_sems, corner_sems,
):
    height, width = rows_ref.shape
    stride = flat_ref.shape[0] // height
    row_count, col_count = lax.axis_size("row"), lax.axis_size("col")
    row_place, col_place = lax.axis_index("row"), lax.axis_index("col")
    row_odd, col_odd = lax.rem(row_place, 2), lax.rem(col_place, 2)
    next_col = (row_place, lax.rem(col_place + 2, col_count))
    past_col = (row_place, lax.rem(col_place + col_count - 2, col_count))
    pair_col = (row_place, col_place + 1 - 2 * col_odd)
    next_row = (lax.rem(row_place + 2, row_count), col_place)
    past_row = (lax.rem(row_place + row_count - 2, row_count), col_place)
    pair_row = (row_place + 1 - 2 * row_odd, col_place)

    barrier = pltpu.get_barrier_semaphore()
    friends = (next_col, past_col, pair_col, next_row, past_row, pair_row)
    for friend in friends:
        pl.semaphore_signal(barrier, inc=1, device_id=friend, device_id_type=MESH)

    for k in range(2):

        @pl.when(col_place == k)
        def _():
            for m in range(nb // LANES):
                at = slice(k * nb + m * LANES, k * nb + (m + 1) * LANES)
                rows_ref[:, at] = flat_ref[pl.ds(m, height, stride=stride), :]

        @pl.when(row_place == k)
        def _():
            here = slice(k * nb, (k + 1) * nb)
            for m in range(stride):
                at = slice(m * LANES, (m + 1) * LANES)
                head_ref[here, at] = flat_ref[pl.ds(m, nb, stride=stride), :]
            head_ref[here, stride * LANES :] = jnp.zeros(
                (nb, head_ref.shape[1] - stride * LANES), jnp.float32
            )
            head_ref[here, stride * LANES : stride * LANES + rhs_ref.shape[1]] = rhs_ref[:nb, :]

    pl.semaphore_wait(barrier, len(friends))

    def pass_on(ref, sems, index, place, count, onward, partner):
        first, second, third, fourth = sems
        chain = pltpu.make_async_remote_copy(
            src_ref=ref, dst_ref=ref, send_sem=first.at[index], recv_sem=second.at[index],
            device_id=onward, device_id_type=MESH,
        )
        pair = pltpu.make_async_remote_copy(
            src_ref=ref, dst_ref=ref, send_sem=third.at[index], recv_sem=fourth.at[index],
            device_id=partner, device_id_type=MESH,
        )

        @pl.when(place >= 2)
        def _():
            chain.wait_recv()

        @pl.when(place + 2 < count)
        def _():
            chain.start()

        pair.start()

    def finish(ref, other, sems, index, place, count, onward, partner, received):
        first, second, third, fourth = sems
        chain = pltpu.make_async_remote_copy(
            src_ref=ref, dst_ref=ref, send_sem=first.at[index], recv_sem=second.at[index],
            device_id=onward, device_id_type=MESH,
        )
        pair = pltpu.make_async_remote_copy(
            src_ref=ref, dst_ref=other, send_sem=third.at[index], recv_sem=fourth.at[index],
            device_id=partner, device_id_type=MESH,
        )

        @pl.when(place + 2 < count)
        def _():
            chain.wait_send()

        pair.wait_send()
        if not received:
            pair.wait_recv()

    half = nb // 2
    chunks = height // half
    col_sems = (send_a, recv_a, send_b, recv_b)
    mine = pl.ds(pl.multiple_of(col_odd * nb, nb), nb)
    theirs = pl.ds(pl.multiple_of((1 - col_odd) * nb, nb), nb)
    row_mine = pl.ds(pl.multiple_of(row_odd * nb, nb), nb)
    row_theirs = pl.ds(pl.multiple_of((1 - row_odd) * nb, nb), nb)
    by_col = (col_place, col_count, next_col, pair_col)
    by_row = (row_place, row_count, next_row, pair_row)

    def part(m, columns):
        return rows_ref.at[pl.ds(m * half, half), columns]

    for m in range(2):
        pass_on(part(m, mine), col_sems, m, *by_col)
    head_group = tuple(head_sems.at[j] for j in range(4))
    corner_group = tuple(corner_sems.at[j] for j in range(4))
    for m in range(2):
        pltpu.make_async_remote_copy(
            src_ref=part(m, mine), dst_ref=part(m, theirs), send_sem=send_b.at[m],
            recv_sem=recv_b.at[m], device_id=pair_col, device_id_type=MESH,
        ).wait_recv()

    @pl.when(row_place < 2)
    def _():
        corner_ref[row_mine, :] = rows_ref[:nb, :]

    pass_on(corner_ref.at[row_mine, :], corner_group, 0, *by_row)
    pass_on(part(2, mine), col_sems, 2, *by_col)
    pass_on(head_ref.at[row_mine, :], head_group, 0, *by_row)
    for m in range(3, chunks):
        pass_on(part(m, mine), col_sems, m, *by_col)
    finish(corner_ref.at[row_mine, :], corner_ref.at[row_theirs, :], corner_group, 0, *by_row, False)
    finish(head_ref.at[row_mine, :], head_ref.at[row_theirs, :], head_group, 0, *by_row, False)
    for m in range(chunks):
        finish(part(m, mine), part(m, theirs), col_sems, m, *by_col, m < 2)


def spread(nb, flat, rhs, height, width):
    vmem = pl.BlockSpec(memory_space=pltpu.VMEM)
    room = width + -(-rhs.shape[1] // LANES) * LANES
    chunks = height // (nb // 2)
    dma = pltpu.SemaphoreType.DMA
    return pl.pallas_call(
        functools.partial(spread_kernel, nb),
        out_shape=(
            jax.ShapeDtypeStruct((height, 2 * nb), jnp.float32),
            jax.ShapeDtypeStruct((2 * nb, 2 * nb), jnp.float32),
            jax.ShapeDtypeStruct((2 * nb, room), jnp.float32),
        ),
        in_specs=[vmem] * 2,
        out_specs=(vmem,) * 3,
        scratch_shapes=[dma((chunks,))] * 4 + [dma((4, 1))] * 2,
        compiler_params=pltpu.CompilerParams(
            vmem_limit_bytes=40 * 1024 * 1024, collective_id=0, has_side_effects=True
        ),
    )(flat, rhs)


def compute_kernel(
    nb, corner_ref, head_ref, rows_ref, own_ref, own_rhs_ref, out_ref, out_rhs_ref,
    work, cols, inverse_ref, panel,
):
    size = corner_ref.shape[0]
    steps = size // BASE
    stride = own_ref.shape[0] // rows_ref.shape[0]
    width = stride * LANES
    rhs_width = own_rhs_ref.shape[1]
    row_blocks = rows_ref.shape[0] // nb
    row_count = lax.axis_size("row")
    row_place = lax.axis_index("row")
    col_place = lax.axis_index("col")
    work[...] = corner_ref[...]
    cols[...] = head_ref[...]
    for b in range(steps):
        at = slice(b * BASE, (b + 1) * BASE)
        inverse = base_inverse(work[at, at])
        inverse_ref[at, :] = inverse
        cols[at, :] = exact_dot(inverse, cols[at, :], ((1,), (0,)))
        if b == steps - 1:
            break
        rest = slice((b + 1) * BASE, size)
        upper = exact_dot(inverse, work[at, rest], ((1,), (0,)))
        work[at, rest] = upper
        work[rest, rest] = work[rest, rest] - exact_dot(upper, upper, ((0,), (0,)))
        cols[rest, :] = cols[rest, :] - exact_dot(upper, cols[at, :], ((0,), (0,)))
    solved = halves(cols[...])
    row_in = lax.broadcasted_iota(jnp.int32, (nb, nb), 0)
    col_in = lax.broadcasted_iota(jnp.int32, (nb, nb), 1)
    for rb in range(row_blocks):
        block_row = rb * row_count + row_place
        rows = slice(rb * nb, (rb + 1) * nb)
        for b in range(steps):
            at = slice(b * BASE, (b + 1) * BASE)
            value = rows_ref[rows, at]
            if b:
                value = value - exact_dot(panel[rows, : b * BASE], work[: b * BASE, at], ((1,), (0,)))
            panel[rows, at] = exact_dot(value, inverse_ref[at, :], ((1,), (1,)))
        if rb == 0:
            for k in range(2):
                at = slice(k * nb, (k + 1) * nb)
                keep = (block_row > k) | ((block_row == k) & (row_in >= col_in))
                panel[rows, at] = jnp.where(keep, panel[rows, at], 0.0)
            left = jnp.concatenate(
                [
                    jnp.where(block_row > k, panel[rows, k * nb : (k + 1) * nb], 0.0)
                    for k in range(2)
                ],
                axis=1,
            )
        else:
            left = panel[rows, :]
        product = split_dot(halves(left), solved, ((1,), (0,)))
        for m in range(stride):
            spot = pl.ds(rb * nb * stride + m, nb, stride=stride)
            out_ref[spot, :] = own_ref[spot, :] - product[:, m * LANES : (m + 1) * LANES]
        rhs_now = own_rhs_ref[rows, :] - product[:, width : width + rhs_width]
        if rb == 0:
            for k in range(2):
                rhs_now = jnp.where(block_row == k, cols[k * nb : (k + 1) * nb, width : width + rhs_width], rhs_now)
        out_rhs_ref[rows, :] = rhs_now
        for k in range(2):

            @pl.when(col_place == k)
            def _():
                for m in range(nb // LANES):
                    spot = pl.ds(rb * nb * stride + m, nb, stride=stride)
                    at = slice(k * nb + m * LANES, k * nb + (m + 1) * LANES)
                    out_ref[spot, :] = panel[rows, at]


def compute(nb, corner, head, rows, own, own_rhs):
    size = corner.shape[0]
    vmem = pl.BlockSpec(memory_space=pltpu.VMEM)
    return pl.pallas_call(
        functools.partial(compute_kernel, nb),
        out_shape=(
            jax.ShapeDtypeStruct(own.shape, jnp.float32),
            jax.ShapeDtypeStruct(own_rhs.shape, jnp.float32),
        ),
        in_specs=[vmem] * 5,
        out_specs=(vmem, vmem),
        scratch_shapes=[
            pltpu.VMEM((size, size), jnp.float32),
            pltpu.VMEM(head.shape, jnp.float32),
            pltpu.VMEM((size, BASE), jnp.float32),
            pltpu.VMEM(rows.shape, jnp.float32),
        ],
        compiler_params=pltpu.CompilerParams(vmem_limit_bytes=48 * 1024 * 1024),
    )(corner, head, rows, own, own_rhs)


def shards(kernel, targets):
    row_blocks, nb, col_blocks = kernel.shape[0], kernel.shape[2], kernel.shape[3]
    width = targets.shape[3]
    height, breadth = row_blocks * nb, col_blocks * nb
    own = kernel.reshape(height * breadth // LANES, LANES)
    own_rhs = targets.reshape(height, width)
    rows, corner, head = spread(nb, own, own_rhs, height, breadth)
    out, out_rhs = compute(nb, corner, head, rows, own, own_rhs)
    return out.reshape(kernel.shape), out_rhs.reshape(targets.shape)


def solution(mesh):
    return jax.shard_map(
        shards,
        mesh=mesh,
        in_specs=(P(None, "row", None, None, "col", None), P(None, "row", None, "col")),
        out_specs=(P(None, "row", None, None, "col", None), P(None, "row", None, "col")),
        check_vma=False,
    )
```

profile of v0, /device:TPU:28, one launch (start us, length us, event | category | flops | bytes accessed | tf_op | source)
XLA Modules:
  0.0 107.7 jit_solution(15012159889553380789)
XLA Ops:
  0.6 1.1 %copy.4 = f32[4,1,256,64]{3,2,0,1:T(8,128)S(1)} copy(f32[4,1,256,64]{2,3,1,0:T(8,128)} %param.3) | data formatting | bytes 524288 | tf_op args[1]
  1.8 0.0 copy-start
  1.8 1.6 %copy-done = f32[4,1,256,2,1,256]{5,4,3,2,1,0:T(1,128)S(1)} copy-done((f32[4,1,256,2,1,256]{5,4,3,2,1,0:T(1,128)S(1)}, f32[4,1,256,2,1,256]{5,4,3,2,1,0:T(1,128)}, u32[]{:S(2)}) %copy-start) | copy-done | bytes 2097176
  3.4 63.7 %shard_map.41 = (f32[1024,512]{1,0:T(8,128)S(1)}, f32[512,512]{1,0:T(8,128)S(1)}, f32[512,640]{1,0:T(8,128)S(1)}) custom-call(f32[4096,128]{1,0:T(8,128)S(1)} %bitcast.5, f32[1024,64]{1,0:T(8,128)S(1)} %bitcast.6), custom_call_target="tpu_custom_call" | custom-call | tf_op jit(solution)/shard_map/pallas_call | solution.py:218
  67.1 39.7 %shard_map.42 = (f32[4096,128]{1,0:T(8,128)}, f32[1024,64]{1,0:T(8,128)S(1)}) custom-call(f32[512,512]{1,0:T(8,128)S(1)} %get-tuple-element.7.corner_ref, f32[512,640]{1,0:T(8,128)S(1)} %get-tuple-element.8.head_ref, f32[1024,512]{1,0:T(8,128)S(1)} %get-tuple-element.9.rows_ref, f32[4096,128]{1,0:T(8,128)} %bitcast.4, f32[1024,64]{1,0:T(8,128)S(1)} %bitcast.7), custom_call_target="tpu_custom_call" | custom-call | tf_op jit(solution)/shard_map/pallas_call | solution.py:309
  106.8 0.9 copy.6
Async XLA Ops:
  1.8 1.6 %copy-start = (f32[4,1,256,2,1,256]{5,4,3,2,1,0:T(1,128)S(1)}, f32[4,1,256,2,1,256]{5,4,3,2,1,0:T(1,128)}, u32[]{:S(2)}) copy-start(f32[4,1,256,2,1,256]{5,4,3,2,1,0:T(1,128)} %param.2) | copy-start | bytes 6291460
where the time goes:
time: 108 us
  Pallas kernels  103 us (95%)
  local copies, waits for them, and re-layouts  3.62 us (3%)
    pallas_call x1, Pallas kernels, spread(): pl.pallas_call(functools.partial(spread_kernel, nb), out_shape=(jax.Shape...  63.7 us
    pallas_call x1, Pallas kernels, compute(): pl.pallas_call(functools.partial(compute_kernel, nb), out_shape=(jax.Shap...  39.7 us
    unnamed x4, local copies, waits for them, and re-layouts  3.62 us

commit v1 on v0

--- a/solution.py
+++ b/solution.py
@@ -32,7 +32,7 @@
     return dot(a_high, b_high) + (dot(a_high, b_low) + dot(a_low, b_high))
 
 
-def base_inverse(block):
+def base_inverse(block, between):
     groups = BASE // STEP
     rows = lax.broadcasted_iota(jnp.int32, (STEP, BASE), 0)
     lanes = lax.broadcasted_iota(jnp.int32, (STEP, BASE), 1)
@@ -66,6 +66,8 @@
         for k in range(STEP):
             scaled = jnp.where(rows == k, sides[k] * lax.rsqrt(spot[k][k]), scaled)
         done.append(scaled)
+        if q % 4 == 3:
+            between()
         if q == groups - 1:
             break
         mains = [mains[k] * recips[k] for k in range(STEP)]
@@ -90,8 +92,9 @@
 LANES = 128
 
 
-def spread_kernel(
-    nb, flat_ref, rhs_ref, rows_ref, corner_ref, head_ref,
+def fused_kernel(
+    nb, flat_ref, rhs_ref, out_ref, out_rhs_ref,
+    rows_ref, corner_ref, head_ref, work, cols, inverse_ref, panel,
     send_a, recv_a, send_b, recv_b, head_sems, corner_sems,
 ):
     height, width = rows_ref.shape
@@ -200,55 +203,36 @@
         corner_ref[row_mine, :] = rows_ref[:nb, :]
 
     pass_on(corner_ref.at[row_mine, :], corner_group, 0, *by_row)
-    pass_on(part(2, mine), col_sems, 2, *by_col)
-    pass_on(head_ref.at[row_mine, :], head_group, 0, *by_row)
-    for m in range(3, chunks):
-        pass_on(part(m, mine), col_sems, m, *by_col)
     finish(corner_ref.at[row_mine, :], corner_ref.at[row_theirs, :], corner_group, 0, *by_row, False)
-    finish(head_ref.at[row_mine, :], head_ref.at[row_theirs, :], head_group, 0, *by_row, False)
-    for m in range(chunks):
-        finish(part(m, mine), part(m, theirs), col_sems, m, *by_col, m < 2)
-
-
-def spread(nb, flat, rhs, height, width):
-    vmem = pl.BlockSpec(memory_space=pltpu.VMEM)
-    room = width + -(-rhs.shape[1] // LANES) * LANES
-    chunks = height // (nb // 2)
-    dma = pltpu.SemaphoreType.DMA
-    return pl.pallas_call(
-        functools.partial(spread_kernel, nb),
-        out_shape=(
-            jax.ShapeDtypeStruct((height, 2 * nb), jnp.float32),
-            jax.ShapeDtypeStruct((2 * nb, 2 * nb), jnp.float32),
-            jax.ShapeDtypeStruct((2 * nb, room), jnp.float32),
-        ),
-        in_specs=[vmem] * 2,
-        out_specs=(vmem,) * 3,
-        scratch_shapes=[dma((chunks,))] * 4 + [dma((4, 1))] * 2,
-        compiler_params=pltpu.CompilerParams(
-            vmem_limit_bytes=40 * 1024 * 1024, collective_id=0, has_side_effects=True
-        ),
-    )(flat, rhs)
-
-
-def compute_kernel(
-    nb, corner_ref, head_ref, rows_ref, own_ref, own_rhs_ref, out_ref, out_rhs_ref,
-    work, cols, inverse_ref, panel,
-):
+    events = {}
+    events[1] = lambda: pass_on(head_ref.at[row_mine, :], head_group, 0, *by_row)
+    for m in range(2, chunks):
+        slot = 0 if m == 2 else 2 * m - 3
+        events[slot] = functools.partial(pass_on, part(m, mine), col_sems, m, *by_col)
+    order = [events[slot] for slot in sorted(events)]
+    slots = sorted(events)
+    passed = [0, 0]
+
+    def between():
+        while passed[1] < len(order) and slots[passed[1]] <= passed[0]:
+            order[passed[1]]()
+            passed[1] += 1
+        passed[0] += 1
+
     size = corner_ref.shape[0]
     steps = size // BASE
-    stride = own_ref.shape[0] // rows_ref.shape[0]
     width = stride * LANES
-    rhs_width = own_rhs_ref.shape[1]
+    rhs_width = rhs_ref.shape[1]
     row_blocks = rows_ref.shape[0] // nb
-    row_count = lax.axis_size("row")
-    row_place = lax.axis_index("row")
-    col_place = lax.axis_index("col")
     work[...] = corner_ref[...]
-    cols[...] = head_ref[...]
     for b in range(steps):
         at = slice(b * BASE, (b + 1) * BASE)
-        inverse = base_inverse(work[at, at])
+        inverse = base_inverse(work[at, at], between)
+        if b == 0:
+            finish(
+                head_ref.at[row_mine, :], head_ref.at[row_theirs, :], head_group, 0, *by_row, False
+            )
+            cols[...] = head_ref[...]
         inverse_ref[at, :] = inverse
         cols[at, :] = exact_dot(inverse, cols[at, :], ((1,), (0,)))
         if b == steps - 1:
@@ -258,6 +242,10 @@
         work[at, rest] = upper
         work[rest, rest] = work[rest, rest] - exact_dot(upper, upper, ((0,), (0,)))
         cols[rest, :] = cols[rest, :] - exact_dot(upper, cols[at, :], ((0,), (0,)))
+    while passed[1] < len(order):
+        between()
+    for m in range(chunks):
+        finish(part(m, mine), part(m, theirs), col_sems, m, *by_col, m < 2)
     solved = halves(cols[...])
     row_in = lax.broadcasted_iota(jnp.int32, (nb, nb), 0)
     col_in = lax.broadcasted_iota(jnp.int32, (nb, nb), 1)
@@ -287,8 +275,8 @@
         product = split_dot(halves(left), solved, ((1,), (0,)))
         for m in range(stride):
             spot = pl.ds(rb * nb * stride + m, nb, stride=stride)
-            out_ref[spot, :] = own_ref[spot, :] - product[:, m * LANES : (m + 1) * LANES]
-        rhs_now = own_rhs_ref[rows, :] - product[:, width : width + rhs_width]
+            out_ref[spot, :] = flat_ref[spot, :] - product[:, m * LANES : (m + 1) * LANES]
+        rhs_now = rhs_ref[rows, :] - product[:, width : width + rhs_width]
         if rb == 0:
             for k in range(2):
                 rhs_now = jnp.where(block_row == k, cols[k * nb : (k + 1) * nb, width : width + rhs_width], rhs_now)
@@ -303,25 +291,35 @@
                     out_ref[spot, :] = panel[rows, at]
 
 
-def compute(nb, corner, head, rows, own, own_rhs):
-    size = corner.shape[0]
+def fused(nb, flat, rhs, height, width):
     vmem = pl.BlockSpec(memory_space=pltpu.VMEM)
+    room = width + -(-rhs.shape[1] // LANES) * LANES
+    size = 2 * nb
+    chunks = height // (nb // 2)
+    dma = pltpu.SemaphoreType.DMA
     return pl.pallas_call(
-        functools.partial(compute_kernel, nb),
+        functools.partial(fused_kernel, nb),
         out_shape=(
-            jax.ShapeDtypeStruct(own.shape, jnp.float32),
-            jax.ShapeDtypeStruct(own_rhs.shape, jnp.float32),
+            jax.ShapeDtypeStruct(flat.shape, jnp.float32),
+            jax.ShapeDtypeStruct(rhs.shape, jnp.float32),
         ),
-        in_specs=[vmem] * 5,
+        in_specs=[vmem] * 2,
         out_specs=(vmem, vmem),
         scratch_shapes=[
+            pltpu.VMEM((height, size), jnp.float32),
             pltpu.VMEM((size, size), jnp.float32),
-            pltpu.VMEM(head.shape, jnp.float32),
+            pltpu.VMEM((size, room), jnp.float32),
+            pltpu.VMEM((size, size), jnp.float32),
+            pltpu.VMEM((size, room), jnp.float32),
             pltpu.VMEM((size, BASE), jnp.float32),
-            pltpu.VMEM(rows.shape, jnp.float32),
+            pltpu.VMEM((height, size), jnp.float32),
+            *[dma((chunks,))] * 4,
+            *[dma((4, 1))] * 2,
         ],
-        compiler_params=pltpu.CompilerParams(vmem_limit_bytes=48 * 1024 * 1024),
-    )(corner, head, rows, own, own_rhs)
+        compiler_params=pltpu.CompilerParams(
+            vmem_limit_bytes=48 * 1024 * 1024, collective_id=0, has_side_effects=True
+        ),
+    )(flat, rhs)
 
 
 def shards(kernel, targets):
@@ -330,8 +328,7 @@
     height, breadth = row_blocks * nb, col_blocks * nb
     own = kernel.reshape(height * breadth // LANES, LANES)
     own_rhs = targets.reshape(height, width)
-    rows, corner, head = spread(nb, own, own_rhs, height, breadth)
-    out, out_rhs = compute(nb, corner, head, rows, own, own_rhs)
+    out, out_rhs = fused(nb, own, own_rhs, height, breadth)
     return out.reshape(kernel.shape), out_rhs.reshape(targets.shape)
 
 

time: 108 us -> 93.3 us (0.86)
  Pallas kernels: 103 us -> 87.6 us
  local copies, waits for them, and re-layouts: 3.62 us -> 4.94 us
    pallas_call x2 -> x1, Pallas kernels: 103 us -> 87.6 us  [fused(): pl.pallas_call(functools.partial(fused_kernel, nb), out_shape=(jax.ShapeD...]
    unnamed x4 -> x5, local copies, waits for them, and re-layouts: 3.62 us -> 4.94 us
where the time goes in v1:
time: 93.3 us; the launch traced here: 93.2 us
  Pallas kernels  87.6 us (94%)
  local copies, waits for them, and re-layouts  4.94 us (5%)
    pallas_call x1, Pallas kernels, fused(): pl.pallas_call(functools.partial(fused_kernel, nb), out_shape=(jax.ShapeD...  87.6 us
    unnamed x5, local copies, waits for them, and re-layouts  4.94 us

profile of v1, /device:TPU:28, one launch (start us, length us, event | category | flops | bytes accessed | tf_op | source)
XLA Modules:
  0.0 93.2 jit_solution(11191639193437335436)
XLA Ops:
  0.6 1.1 %copy.4 = f32[4,1,256,64]{3,2,0,1:T(8,128)S(1)} copy(f32[4,1,256,64]{2,3,1,0:T(8,128)} %param.3) | data formatting | bytes 524288 | tf_op args[1]
  1.8 0.0 copy-start
  1.8 1.6 %copy-done = f32[4,1,256,2,1,256]{5,4,3,2,1,0:T(1,128)S(1)} copy-done((f32[4,1,256,2,1,256]{5,4,3,2,1,0:T(1,128)S(1)}, f32[4,1,256,2,1,256]{5,4,3,2,1,0:T(1,128)}, u32[]{:S(2)}) %copy-start) | copy-done | bytes 2097176
  3.4 87.6 %shard_map.41 = (f32[4096,128]{1,0:T(8,128)S(1)}, f32[1024,64]{1,0:T(8,128)S(1)}) custom-call(f32[4096,128]{1,0:T(8,128)S(1)} %bitcast.4, f32[1024,64]{1,0:T(8,128)S(1)} %bitcast.5), custom_call_target="tpu_custom_call" | custom-call | tf_op jit(solution)/shard_map/pallas_call | solution.py:300
  91.0 0.9 copy.6
  91.8 1.3 %copy.8 = f32[4,1,256,2,1,256]{5,4,3,2,1,0:T(1,128)} copy(f32[4,1,256,2,1,256]{5,4,3,2,1,0:T(1,128)S(1)} %bitcast.6) | data formatting | bytes 4194304
Async XLA Ops:
  1.8 1.6 %copy-start = (f32[4,1,256,2,1,256]{5,4,3,2,1,0:T(1,128)S(1)}, f32[4,1,256,2,1,256]{5,4,3,2,1,0:T(1,128)}, u32[]{:S(2)}) copy-start(f32[4,1,256,2,1,256]{5,4,3,2,1,0:T(1,128)} %param.2) | copy-start | bytes 6291460

commit v2 on v1

--- a/solution.py
+++ b/solution.py
@@ -192,18 +192,30 @@
         pass_on(part(m, mine), col_sems, m, *by_col)
     head_group = tuple(head_sems.at[j] for j in range(4))
     corner_group = tuple(corner_sems.at[j] for j in range(4))
+    def corner_half(odd, m):
+        return corner_ref.at[pl.ds(pl.multiple_of(odd * nb + m * half, half), half), :]
+
     for m in range(2):
         pltpu.make_async_remote_copy(
             src_ref=part(m, mine), dst_ref=part(m, theirs), send_sem=send_b.at[m],
             recv_sem=recv_b.at[m], device_id=pair_col, device_id_type=MESH,
         ).wait_recv()
 
-    @pl.when(row_place < 2)
-    def _():
-        corner_ref[row_mine, :] = rows_ref[:nb, :]
-
-    pass_on(corner_ref.at[row_mine, :], corner_group, 0, *by_row)
-    finish(corner_ref.at[row_mine, :], corner_ref.at[row_theirs, :], corner_group, 0, *by_row, False)
+        @pl.when(row_place < 2)
+        def _():
+            corner_half(row_odd, m)[...] = part(m, slice(None))[...]
+
+        pass_on(corner_half(row_odd, m), corner_group, m, *by_row)
+
+    def take_corner(m):
+        finish(
+            corner_half(row_odd, m), corner_half(1 - row_odd, m), corner_group, m, *by_row, False
+        )
+        for k in range(2):
+            at = slice(k * nb + m * half, k * nb + (m + 1) * half)
+            work[at, :] = corner_ref[at, :]
+
+    take_corner(0)
     events = {}
     events[1] = lambda: pass_on(head_ref.at[row_mine, :], head_group, 0, *by_row)
     for m in range(2, chunks):
@@ -224,11 +236,11 @@
     width = stride * LANES
     rhs_width = rhs_ref.shape[1]
     row_blocks = rows_ref.shape[0] // nb
-    work[...] = corner_ref[...]
     for b in range(steps):
         at = slice(b * BASE, (b + 1) * BASE)
         inverse = base_inverse(work[at, at], between)
         if b == 0:
+            take_corner(1)
             finish(
                 head_ref.at[row_mine, :], head_ref.at[row_theirs, :], head_group, 0, *by_row, False
             )
@@ -314,7 +326,8 @@
             pltpu.VMEM((size, BASE), jnp.float32),
             pltpu.VMEM((height, size), jnp.float32),
             *[dma((chunks,))] * 4,
-            *[dma((4, 1))] * 2,
+            dma((4, 1)),
+            dma((4, 2)),
         ],
         compiler_params=pltpu.CompilerParams(
             vmem_limit_bytes=48 * 1024 * 1024, collective_id=0, has_side_effects=True

time: 93.3 us -> 87.6 us (0.939)
  Pallas kernels: 87.6 us -> 81.8 us
    pallas_call x1, Pallas kernels: 87.6 us -> 81.8 us  [fused(): pl.pallas_call(functools.partial(fused_kernel, nb), out_shape=(jax.ShapeD...]
where the time goes in v2:
time: 87.6 us; the launch traced here: 87.4 us
  Pallas kernels  81.8 us (93%)
  local copies, waits for them, and re-layouts  4.94 us (6%)
    pallas_call x1, Pallas kernels, fused(): pl.pallas_call(functools.partial(fused_kernel, nb), out_shape=(jax.ShapeD...  81.8 us
    unnamed x5, local copies, waits for them, and re-layouts  4.94 us

profile of v2, /device:TPU:28, one launch (start us, length us, event | category | flops | bytes accessed | tf_op | source)
XLA Modules:
  0.0 87.4 jit_solution(17051911531631030748)
XLA Ops:
  0.6 1.1 %copy.4 = f32[4,1,256,64]{3,2,0,1:T(8,128)S(1)} copy(f32[4,1,256,64]{2,3,1,0:T(8,128)} %param.3) | data formatting | bytes 524288 | tf_op args[1]
  1.8 0.0 copy-start
  1.8 1.6 %copy-done = f32[4,1,256,2,1,256]{5,4,3,2,1,0:T(1,128)S(1)} copy-done((f32[4,1,256,2,1,256]{5,4,3,2,1,0:T(1,128)S(1)}, f32[4,1,256,2,1,256]{5,4,3,2,1,0:T(1,128)}, u32[]{:S(2)}) %copy-start) | copy-done | bytes 2097176
  3.4 81.8 %shard_map.41 = (f32[4096,128]{1,0:T(8,128)S(1)}, f32[1024,64]{1,0:T(8,128)S(1)}) custom-call(f32[4096,128]{1,0:T(8,128)S(1)} %bitcast.4, f32[1024,64]{1,0:T(8,128)S(1)} %bitcast.5), custom_call_target="tpu_custom_call" | custom-call | tf_op jit(solution)/shard_map/pallas_call | solution.py:312
  85.2 0.9 %copy.6 = f32[4,1,256,64]{2,3,1,0:T(8,128)} copy(f32[4,1,256,64]{3,2,0,1:T(8,128)S(1)} %bitcast.7) | data formatting | bytes 524288
  86.1 1.3 %copy.8 = f32[4,1,256,2,1,256]{5,4,3,2,1,0:T(1,128)} copy(f32[4,1,256,2,1,256]{5,4,3,2,1,0:T(1,128)S(1)} %bitcast.6) | data formatting | bytes 4194304
Async XLA Ops:
  1.8 1.6 %copy-start = (f32[4,1,256,2,1,256]{5,4,3,2,1,0:T(1,128)S(1)}, f32[4,1,256,2,1,256]{5,4,3,2,1,0:T(1,128)}, u32[]{:S(2)}) copy-start(f32[4,1,256,2,1,256]{5,4,3,2,1,0:T(1,128)} %param.2) | copy-start | bytes 6291460
